TPU v7x, 256 devices: a whole 4x4x8 slice. The times are simulated.
256 devices in a mesh: freq: 16 (over z, core), tcol: 16 (over x, y).
Axes of the slice: x: 4, y: 4, z: 8, core: 2. Of those that a mesh axis runs over, the one named last changes fastest.
Arguments:
- kernel_v: bfloat16 [16, 32, 64, 2, 32, 256], P('freq', None, 'tcol'), may hold values from -0.25 to 0.25
- kernel_u: bfloat16 [16, 32, 64, 2, 32, 256], P('freq', 'tcol'), may hold values from -0.125 to 0.125
- sources: bfloat16 [16, 2, 16384, 256], P('freq', None, 'tcol'), may hold values from -6 to 6
- ranks: int32 [16, 32, 64], P('freq', None, 'tcol'), may hold values from 4 to 32, as said below
- row_owner: int32 [32], replicated, may hold values from 0 to 15, as said below
Outputs:
- seismo: float32 [16, 32, 256, 256], P('freq', 'tcol')
Inputs may be any that keep to these rules, and one draw needn't show every extreme that they name: Ranks are whole numbers; the bounds are reached for every frequency. For every frequency, owner o and index d of tcol, the ranks of the tiles in tile rows owned by o and tile columns d * 4 to (d + 1) * 4 - 1 sum to at most 192, and this total is reached for every frequency. `row_owner`: every index of tcol owns exactly 2 tile rows.
All inputs are finite; a program needn't handle non-finite values.
Results may differ from a plain program's by a relative error of at most 0.0029.
Values may be sent and summed in bfloat16 or wider, within the bound.
A program may use at most 64 MiB of HBM per device.

v0:
```python
import jax
import jax.numpy as jnp
from jax import lax
from jax.sharding import PartitionSpec as P

TIME_DEV = 1


def on_device(kernel_v, kernel_u, sources, ranks, row_owner):
    groups = lax.axis_size("tcol")
    freq_count = lax.axis_size("freq")
    vee = kernel_v[0]
    rows_all, cols_here, parts, slots, tile = vee.shape
    width = sources.shape[-1]
    fields = sources[0].reshape(parts, cols_here, tile, width)
    prod = jnp.einsum("ijarc,bjcs->ijabrs", vee, fields, preferred_element_type=jnp.float32)
    coeff_real = prod[:, :, 0, 0] + prod[:, :, 1, 1]
    coeff_imag = prod[:, :, 0, 1] - prod[:, :, 1, 0]
    keep = (jnp.arange(slots, dtype=jnp.int32)[None, None, :] < ranks[0][:, :, None]).astype(
        jnp.float32
    )
    coeff = (jnp.stack([coeff_real, coeff_imag], axis=2) * keep[:, :, None, :, None]).astype(
        jnp.bfloat16
    )
    keys = row_owner * rows_all + jnp.arange(rows_all, dtype=jnp.int32)
    order = jnp.argsort(keys)
    owned = rows_all // groups
    outgoing = jnp.take(coeff, order, axis=0).reshape(groups, owned, cols_here, parts, slots, width)
    arrived = lax.all_to_all(outgoing, "tcol", split_axis=0, concat_axis=2, tiled=True)[0]
    quad = jnp.einsum(
        "qjart,qjbrs->qabts", kernel_u[0], arrived, preferred_element_type=jnp.float32
    )
    y_real = quad[:, 0, 0] - quad[:, 1, 1]
    y_imag = quad[:, 0, 1] + quad[:, 1, 0]
    total_times = TIME_DEV * freq_count
    scale = freq_count ** (-0.5)
    freq_here = lax.axis_index("freq")
    times = jnp.arange(lax.axis_size("freq") * TIME_DEV, dtype=jnp.int32)
    phase = (freq_here + 1) * times % (2 * total_times)
    angle = jnp.pi * phase.astype(jnp.float32) / total_times
    cos_col = (jnp.cos(angle) * scale)[:, None, None, None]
    sin_col = (jnp.sin(angle) * scale)[:, None, None, None]
    return lax.psum_scatter(
        cos_col * y_real[None] - sin_col * y_imag[None], "freq", scatter_dimension=0, tiled=True
    )


def solution(mesh):
    return jax.shard_map(
        on_device,
        mesh=mesh,
        in_specs=(
            P("freq", None, "tcol", None, None, None),
            P("freq", "tcol", None, None, None, None),
            P("freq", None, "tcol", None),
            P("freq", None, "tcol"),
            P(),
        ),
        out_specs=P("freq", "tcol", None, None),
        check_vma=False,
    )
```

profile of v0, /device:TPU:2, one launch (start us, length us, event | category | flops | bytes accessed | tf_op | source)
XLA Modules:
  0.0 216.0 jit_solution(1375354114752195918)
XLA Ops:
  6.5 4.8 %convolution_bitcast_fusion = f32[32,4,2,2,32,256]{5,4,2,0,3,1:T(8,128)S(1)} fusion(bf16[2,4,256,256,1,1]{3,2,1,0,5,4:T(8,128)(2,1)} %bitcast.50, bf16[1,32,4,2,32,256]{5,4,3,2,1,0:T(8,128)(2,1)} %param.5), kind=kOutput, calls=%fused_computation.1 | convolution fusion | flops 2147483648 | bytes 22020096 | tf_op jit(solution)/shard_map/ijarc,bjcs->ijabrs/dot_general | solution.py:16
  11.4 2.9 %fusion.1 = f32[32,4,1,32,256]{4,3,0,1,2:T(8,128)} fusion(f32[32,4,2,2,32,256]{5,4,2,0,3,1:T(8,128)S(1)} %convolution_bitcast_fusion), kind=kLoop, calls=%fused_computation.6 | loop fusion | flops 1048576 | bytes 12582912 | tf_op jit(solution)/shard_map/sub | solution.py:18
  14.3 0.0 copy-start.1
  14.3 0.0 copy-start
  14.3 2.9 %fusion.3 = f32[32,4,1,32,256]{4,3,0,1,2:T(8,128)} fusion(f32[32,4,2,2,32,256]{5,4,2,0,3,1:T(8,128)S(1)} %convolution_bitcast_fusion), kind=kLoop, calls=%fused_computation.9 | loop fusion | flops 1048576 | bytes 12582912 | tf_op jit(solution)/shard_map/add | solution.py:17
  17.2 0.0 copy-done.1
  17.2 1.6 sort.17
  18.8 0.0 copy-done
  18.8 0.1 fusion.16
  18.9 0.1 broadcast_in_dim.20
  19.0 5.2 %fusion = bf16[32,4,2,32,256]{4,3,0,1,2:T(8,128)(2,1)} fusion(f32[32,4,1,32,256]{4,3,0,1,2:T(8,128)} %fusion.1, f32[32,4,1,32,256]{4,3,0,1,2:T(8,128)} %fusion.3, f32[32,4,32]{2,0,1:T(8,128)S(1)} %fusion.16), kind=kLoop, calls=%fused_computation.3 | loop fusion | flops 6291456 | bytes 12599296 | tf_op jit(solution)/shard_map/convert_element_type | solution.py:22
  24.3 5.0 %gather_fusion = bf16[32,4,2,32,256]{4,3,1,2,0:T(8,128)(2,1)} fusion(bf16[32,4,2,32,256]{4,3,0,1,2:T(8,128)(2,1)} %fusion, s32[1024]{0:T(1024)S(1)} %pad_clamp_fusion), kind=kCustom, calls=%fused_computation | custom fusion | bytes 8388736 | tf_op jit(solution)/shard_map/jit(_take)/gather | solution.py:28
  29.2 4.6 %broadcast_select_fusion = bf16[16,2,4,2,32,256]{5,4,2,3,1,0:T(8,128)(2,1)} fusion(bf16[16,2,4,2,32,256]{5,4,2,3,1,0:T(8,128)(2,1)} %bitcast.49, pred[16,2]{1,0:T(8,128)(4,1)S(1)} %broadcast_in_dim.20), kind=kLoop, calls=%fused_computation.15 | loop fusion | flops 2097152 | bytes 8388640 | tf_op jit(solution)/shard_map/jit(_take)/select_n | solution.py:28
  33.9 7.5 %all-to-all-start = ((bf16[16,2,4,2,32,256]{5,4,2,3,1,0:T(8,128)(2,1)}), bf16[16,2,4,2,32,256]{5,4,2,3,1,0:T(8,128)(2,1)}, u32[]{:S(2)}, u32[]{:S(2)}) async-start(bf16[16,2,4,2,32,256]{5,4,2,3,1,0:T(8,128)(2,1)} %broadcast_select_fusion), calls=%async_computation | async-start | bytes 8388608 | tf_op jit(solution)/shard_map/all_to_all | solution.py:29
  41.3 0.2 reduce-scatter.2.cloned.1.call-start
  41.6 0.1 sine_multiply_fusion
  41.6 54.0 %all-to-all-done = bf16[16,2,4,2,32,256]{5,4,2,3,1,0:T(8,128)(2,1)} async-done(((bf16[16,2,4,2,32,256]{5,4,2,3,1,0:T(8,128)(2,1)}), bf16[16,2,4,2,32,256]{5,4,2,3,1,0:T(8,128)(2,1)}, u32[]{:S(2)}, u32[]{:S(2)}) %all-to-all-start) | async-done | bytes 4194336 | tf_op jit(solution)/shard_map/all_to_all | solution.py:29
  95.6 7.4 %copy.18 = bf16[1,2,16,4,2,32,256]{6,3,2,5,4,1,0:T(4,128)(2,1)} copy(bf16[1,2,16,4,2,32,256]{6,5,3,4,1,2,0:T(8,128)(2,1)} %bitcast.10) | data formatting | bytes 8388608 | tf_op jit(solution)/shard_map/all_to_all | solution.py:29
  103.0 6.9 %reshape.105 = bf16[2,64,2,32,256,1]{4,1,3,2,0,5:T(8,128)(2,1)} reshape(bf16[1,2,16,4,2,32,256]{6,3,2,5,4,1,0:T(4,128)(2,1)} %copy.18) | data formatting | bytes 8388608 | tf_op jit(solution)/shard_map/squeeze | solution.py:29
  109.9 9.2 %fusion.8 = f32[2,2,2,256,256]{3,4,1,2,0:T(8,128)S(1)} fusion(bf16[2,64,2,32,256,1]{4,3,2,1,0,5:T(8,128)(2,1)} %bitcast.52, bf16[2,64,2,32,256,1]{4,1,3,2,0,5:T(8,128)(2,1)} %reshape.105), kind=kOutput, calls=%fused_computation.16 | convolution fusion | flops 2147483648 | bytes 10485760 | tf_op jit(solution)/shard_map/qjart,qjbrs->qabts/dot_general | solution.py:30
  119.2 0.1 fusion.15
  119.3 0.2 copy.20
  119.5 0.2 copy.21
  119.7 4.4 %multiply_subtract_fusion = f32[16,2,256,256]{3,2,1,0:T(8,128)} fusion(f32[2,256,256]{2,1,0:T(8,128)S(1)} %copy.21, f32[16]{0:T(128)S(1)} %get-tuple-element.9, f32[2,256,256]{2,1,0:T(8,128)S(1)} %copy.20, f32[16]{0:T(128)S(1)} %get-tuple-element.10), kind=kLoop, calls=%fused_computation.4 | loop fusion | flops 6291456 | bytes 9437312 | tf_op jit(solution)/shard_map/sub | solution.py:44
  124.2 0.0 reduce-scatter.2.cloned.1.call-update
  124.2 85.0 %reduce-scatter.2.cloned.1.call-done = f32[1,2,256,256]{3,2,1,0:T(8,128)} async-done(((f32[16,2,256,256]{3,2,1,0:T(8,128)}), f32[1,2,256,256]{3,2,1,0:T(8,128)}) %reduce-scatter.2.cloned.1.call-update) | async-done | bytes 524304 | tf_op jit(solution)/shard_map/reduce_scatter | solution.py:43
  (5 shorter events, 0.0 us)
Async XLA Ops:
  14.3 2.9 %copy-start.1 = (s32[32]{0:T(128)S(1)}, s32[32]{0:T(128)}, u32[]{:S(2)}) copy-start(s32[32]{0:T(128)} %param.9) | copy-start | bytes 388
  14.3 4.5 %copy-start = (s32[1,32,4]{1,2,0:T(4,128)S(1)}, s32[1,32,4]{1,2,0:T(4,128)}, u32[]{:S(2)}) copy-start(s32[1,32,4]{1,2,0:T(4,128)} %param.8) | copy-start | bytes 1540
  33.9 61.8 %all-to-all-start = ((bf16[16,2,4,2,32,256]{5,4,2,3,1,0:T(8,128)(2,1)}), bf16[16,2,4,2,32,256]{5,4,2,3,1,0:T(8,128)(2,1)}, u32[]{:S(2)}, u32[]{:S(2)}) async-start(bf16[16,2,4,2,32,256]{5,4,2,3,1,0:T(8,128)(2,1)} %broadcast_select_fusion), calls=%async_computation | async-start | bytes 8388608 | tf_op jit(solution)/shard_map/all_to_all | solution.py:29
  41.3 167.9 %reduce-scatter.2.cloned.1.call-start = ((), (), s32[]{:S(2)}) async-start(), calls=%async_computation.2 | async-start | bytes 8912896 | tf_op jit(solution)/shard_map/reduce_scatter | solution.py:43
Sparse Core Ops, SparseCore 0:
  124.3 84.8 reduce-scatter.1
where the time goes:
time: 216 us
  waiting for transfers between devices  139 us (64%)
  other arithmetic  22 us (10%)
  local copies, waits for them, and re-layouts  19.8 us (9%)
  matrix products  14.1 us (7%)
  between operations  13.5 us (6%)
  starting transfers between devices  7.7 us (4%)
    reduce_scatter x1, waiting for transfers between devices, on_device(): lax.psum_scatter(cos_col * y_real[None] - sin_col * y_imag[None], 'freq',...  85 us
    all_to_all x1, waiting for transfers between devices, on_device(): lax.all_to_all(outgoing, 'tcol', split_axis=0, concat_axis=2, tiled=True)[0]  54 us
    dot_general x1, matrix products, on_device(): jnp.einsum('qjart,qjbrs->qabts', kernel_u[0], arrived, preferred_element_...  9.22 us
    all_to_all x1, starting transfers between devices, on_device(): lax.all_to_all(outgoing, 'tcol', split_axis=0, concat_axis=2, tiled=True)[0]  7.48 us
    all_to_all x1, local copies, waits for them, and re-layouts, on_device(): lax.all_to_all(outgoing, 'tcol', split_axis=0, concat_axis=2, tiled=True)[0]  7.39 us
    squeeze x1, local copies, waits for them, and re-layouts, on_device(): lax.all_to_all(outgoing, 'tcol', split_axis=0, concat_axis=2, tiled=True)[0]  6.93 us
    convert_element_type x1, other arithmetic, on_device(): (jnp.stack([coeff_real, coeff_imag], axis=2) * keep[:, :, None, :, None])...  5.22 us
    gather x1, local copies, waits for them, and re-layouts, on_device(): jnp.take(coeff, order, axis=0)  4.97 us
  transfers between devices with their start and end apart: 2, of which 2 were waited for; matrix products, arithmetic and copies ran while one was open for 0% of the time, Pallas kernels for 0%

commit v1 on v0

v1 whole, which is shorter than its diff:
```python
import jax
import jax.numpy as jnp
from jax import lax
from jax.experimental import pallas as pl
from jax.experimental.pallas import tpu as pltpu
from jax.sharding import PartitionSpec as P

MESH = pl.DeviceIdType.MESH
NX, NY, NZ = 4, 4, 8
GROUPS = NX * NY
ROWS, COLS, SLOTS, TILE, WIDTH = 32, 4, 32, 256, 256
OWN = ROWS // GROUPS
PACK = 192
CHUNKS = 4
HALF = WIDTH // CHUNKS
LANES = 2 * HALF
DEPTH = GROUPS * PACK
LONG, SHORT = 4, 3

OFFSETS = (
    (2, 2), (2, 1), (1, 2), (2, 3), (3, 2), (1, 1), (3, 3), (1, 3), (3, 1),
    (2, 0), (0, 2), (1, 0), (3, 0), (0, 1), (0, 3),
)
PEERS = len(OFFSETS)


def swap_halves(v):
    return pltpu.roll(v, HALF, 1)


def kernel(
    order, table, v_hbm, u_hbm, x_hbm, tgt, out,
    v, u, x, xs, coeff, packed, arrived, heads, left, acc,
    mine, theirs, long_out, long_in, short_out, short_in,
    load_sem, head_send, head_recv, tile_send, tile_recv, pair_send, pair_recv,
    long_send, long_recv, short_send, short_recv,
):
    freq, here = lax.axis_index("freq"), lax.axis_index("tcol")
    z, core = freq // 2, freq % 2
    px, py = here // NY, here % NY

    loads = [
        pltpu.make_async_copy(x_hbm.at[0], x, load_sem.at[0]),
        pltpu.make_async_copy(v_hbm.at[0], v, load_sem.at[1]),
        pltpu.make_async_copy(u_hbm.at[0], u, load_sem.at[2]),
    ]
    for load in loads:
        load.start()

    def peer(k):
        dx, dy = OFFSETS[k]
        return ((px + dx) % NX) * NY + (py + dy) % NY

    sibling = (2 * z + 1 - core, here)
    sigma = 1 - 2 * core
    ahead = (2 * ((z + sigma + NZ) % NZ) + core, here)
    behind = (2 * ((z - sigma + NZ) % NZ) + core, here)

    barrier = pltpu.get_barrier_semaphore()
    partners = [(freq, peer(k)) for k in range(PEERS)] + [sibling, ahead, behind]
    for partner in partners:
        pl.semaphore_signal(barrier, inc=1, device_id=partner, device_id_type=MESH)
    pl.semaphore_wait(barrier, len(partners))

    def remote(src, dst, send, recv, device):
        return pltpu.make_async_remote_copy(
            src_ref=src, dst_ref=dst, send_sem=send, recv_sem=recv,
            device_id=device, device_id_type=MESH,
        )

    head_rows = pl.ds(pl.multiple_of(8 * here, 8), 8)
    head_copies = [
        remote(tgt.at[peer(k)], heads.at[head_rows], head_send.at[k], head_recv.at[k], (freq, peer(k)))
        for k in range(PEERS)
    ]
    for copy in head_copies:
        copy.start()
    heads[head_rows] = tgt[here]

    my_rows = pl.ds(pl.multiple_of(PACK * here, PACK), PACK)

    def tile_copy(c, k):
        return remote(
            packed.at[c, k], arrived.at[c, my_rows], tile_send.at[c, k], tile_recv.at[c, k], (freq, peer(k))
        )

    loads[0].wait()
    first = lax.broadcasted_iota(jnp.int32, (TILE, LANES), 1) < HALF
    rank_row = lax.broadcasted_iota(jnp.int32, (PACK, COLS * SLOTS), 0).astype(jnp.float32)
    for half in range(CHUNKS // 2):
        lanes = pl.ds(half * LANES, LANES)

        @pl.loop(0, COLS)
        def _(j):
            rows = pl.ds(pl.multiple_of(j * TILE, TILE), TILE)
            re = x[0, rows, lanes].astype(jnp.float32)
            im = x[1, rows, lanes].astype(jnp.float32)
            re_swap, im_swap = swap_halves(re), swap_halves(im)
            xs[j, 0, :, :LANES] = jnp.where(first, re, im_swap).astype(jnp.bfloat16)
            xs[j, 0, :, LANES:] = jnp.where(first, re_swap, im).astype(jnp.bfloat16)
            xs[j, 1, :, :LANES] = jnp.where(first, im, -re_swap).astype(jnp.bfloat16)
            xs[j, 1, :, LANES:] = jnp.where(first, im_swap, -re).astype(jnp.bfloat16)

        if half == 0:
            loads[1].wait()

        @pl.loop(0, COLS)
        def _(j):
            slot_rows = pl.ds(pl.multiple_of(j * SLOTS, SLOTS), SLOTS)
            for part in range(2):
                rows = pl.ds(part * (ROWS // 2), ROWS // 2)
                re = v[rows, j, 0].reshape(ROWS // 2 * SLOTS, TILE)
                im = v[rows, j, 1].reshape(ROWS // 2 * SLOTS, TILE)
                prod = jnp.dot(re, xs[j, 0], preferred_element_type=jnp.float32)
                prod += jnp.dot(im, xs[j, 1], preferred_element_type=jnp.float32)
                coeff[rows, slot_rows, :] = prod.astype(jnp.bfloat16).reshape(ROWS // 2, SLOTS, 2 * LANES)

        def pack(owner):
            total = None
            for q in range(OWN):
                pick = jnp.where(rank_row == tgt[owner, q : q + 1, :], 1.0, 0.0).astype(jnp.bfloat16)
                part = jnp.dot(pick, coeff[order[OWN * owner + q]], preferred_element_type=jnp.float32)
                total = part if total is None else total + part
            return total.astype(jnp.bfloat16)

        for k in range(PEERS):
            block = pack(peer(k))
            packed[2 * half, k] = block[:, :LANES]
            packed[2 * half + 1, k] = block[:, LANES:]
            tile_copy(2 * half, k).start()
        for k in range(PEERS):
            tile_copy(2 * half + 1, k).start()
        block = pack(here)
        arrived[2 * half, my_rows] = block[:, :LANES]
        arrived[2 * half + 1, my_rows] = block[:, LANES:]

    for copy in head_copies:
        copy.wait_recv()
    loads[2].wait()
    columns = jnp.transpose(heads[...])
    pair_row = lax.broadcasted_iota(jnp.int32, (COLS * SLOTS, 2 * PACK), 1).astype(jnp.float32)
    for e in range(GROUPS // 2):
        for q in range(OWN):
            sides = []
            for side in range(2):
                at = 8 * (2 * e + side) + q
                column = columns[:, at : at + 1] + float(side * PACK)
                sides.append(jnp.where(pair_row == column, 1.0, 0.0).astype(jnp.bfloat16))
            pick = jnp.concatenate(sides, axis=0)
            for a in range(2):
                block = u[q, 2 * COLS * e : 2 * COLS * (e + 1), a].reshape(2 * COLS * SLOTS, TILE)
                turned = lax.dot_general(block, pick, (((0,), (0,)), ((), ())), preferred_element_type=jnp.float32)
                at = (2 * q + a) * TILE
                left[at : at + TILE, 2 * PACK * e : 2 * PACK * (e + 1)] = turned.astype(jnp.bfloat16)

    for c in range(CHUNKS):
        for k in range(PEERS):
            tile_copy(c, k).wait_recv()
        fields = []
        for q in range(OWN):
            rows = pl.ds(2 * q * TILE, 2 * TILE)
            acc[...] = jnp.dot(left[rows, :], arrived[c], preferred_element_type=jnp.float32)
            turned = swap_halves(acc[TILE:])
            fields.append(acc[:TILE] + jnp.where(first, -turned, turned))
        mine[c, 0] = jnp.where(first, fields[0], swap_halves(fields[1]))
        mine[c, 1] = jnp.where(first, swap_halves(fields[0]), fields[1])
        pair = remote(mine.at[c], theirs.at[c], pair_send.at[c], pair_recv.at[c], sibling)
        pair.start()
        pair.wait_recv()

        def share(steps):
            dest = (z + sigma * steps + NZ) % NZ
            at = (2 * dest + core) * (2 * NZ)
            own, other = at + freq, at + 2 * z + 1 - core
            shift = 4 * NZ * NZ
            return (
                table[own] * mine[c, 0] - table[own + shift] * mine[c, 1]
                + table[other] * theirs[c, 0] - table[other + shift] * theirs[c, 1]
            )

        def long_copy(h):
            return remote(long_out.at[c, h], long_in.at[c, h], long_send.at[c, h], long_recv.at[c, h], ahead)

        def short_copy(h):
            return remote(short_out.at[c, h], short_in.at[c, h], short_send.at[c, h], short_recv.at[c, h], behind)

        for h in range(LONG):
            total = share(LONG - h)
            if h:
                long_copy(h - 1).wait_recv()
                total += long_in[c, h - 1].astype(jnp.float32)
            long_out[c, h] = total.astype(jnp.bfloat16)
            long_copy(h).start()
            if h < SHORT:
                total = share(h - SHORT)
                if h:
                    short_copy(h - 1).wait_recv()
                    total += short_in[c, h - 1].astype(jnp.float32)
                short_out[c, h] = total.astype(jnp.bfloat16)
                short_copy(h).start()
        total = share(0)
        short_copy(SHORT - 1).wait_recv()
        total += short_in[c, SHORT - 1].astype(jnp.float32)
        long_copy(LONG - 1).wait_recv()
        total += long_in[c, LONG - 1].astype(jnp.float32)
        turned = swap_halves(total)
        at = c * HALF
        if c % 2 == 0:
            out[0, 0, :, at : at + HALF] = total[:, :HALF]
            out[0, 1, :, at : at + HALF] = turned[:, :HALF]
        else:
            out[0, 0, :, at : at + HALF] = turned[:, HALF:]
            out[0, 1, :, at : at + HALF] = total[:, HALF:]

        pair.wait_send()
        for h in range(LONG):
            long_copy(h).wait_send()
        for h in range(SHORT):
            short_copy(h).wait_send()
        for k in range(PEERS):
            tile_copy(c, k).wait_send()
    for copy in head_copies:
        copy.wait_send()


def on_device(kernel_v, kernel_u, sources, ranks, row_owner):
    rows = jnp.arange(ROWS, dtype=jnp.int32)
    keys = row_owner * ROWS + rows
    slot = jnp.sum((keys[None, :] < keys[:, None]).astype(jnp.int32), axis=1)
    placed = slot[None, :] == rows[:, None]
    order = jnp.sum(jnp.where(placed, rows[None, :], 0), axis=1)
    slotted = jnp.sum(jnp.where(placed[:, :, None], ranks[0][None], 0), axis=1)
    slotted = slotted.reshape(GROUPS, OWN * COLS)
    tiles = jnp.arange(OWN * COLS, dtype=jnp.int32)
    start = jnp.sum(jnp.where(tiles[None, None, :] < tiles[None, :, None], slotted[:, None, :], 0), axis=2)
    slots = jnp.arange(SLOTS, dtype=jnp.int32)
    target = jnp.where(slots < slotted[:, :, None], start[:, :, None] + slots, -1000)
    target = target.astype(jnp.float32).reshape(GROUPS, OWN, COLS * SLOTS)
    target = jnp.pad(target, ((0, 0), (0, 8 - OWN), (0, 0)), constant_values=-1000.0)

    count = 2 * NZ
    index = jnp.arange(count, dtype=jnp.int32)
    phase = ((index[None, :] + 1) * index[:, None]) % (2 * count)
    angle = jnp.pi * phase.astype(jnp.float32) / count
    scale = count ** (-0.5)
    table = jnp.concatenate([(jnp.cos(angle) * scale).reshape(-1), (jnp.sin(angle) * scale).reshape(-1)])

    bf16, f32 = jnp.bfloat16, jnp.float32
    vmem, dma = pltpu.VMEM, pltpu.SemaphoreType.DMA
    whole = pl.BlockSpec(memory_space=pltpu.VMEM)
    scalars = pl.BlockSpec(memory_space=pltpu.SMEM)
    away = pl.BlockSpec(memory_space=pl.ANY)
    return pl.pallas_call(
        kernel,
        out_shape=jax.ShapeDtypeStruct((1, OWN, TILE, WIDTH), f32),
        in_specs=[scalars, scalars, away, away, away, whole],
        out_specs=whole,
        scratch_shapes=[
            vmem(kernel_v.shape[1:], bf16),
            vmem(kernel_u.shape[1:], bf16),
            vmem(sources.shape[1:], bf16),
            vmem((COLS, 2, TILE, 2 * LANES), bf16),
            vmem((ROWS, COLS * SLOTS, 2 * LANES), bf16),
            vmem((CHUNKS, PEERS, PACK, LANES), bf16),
            vmem((CHUNKS, DEPTH, LANES), bf16),
            vmem((8 * GROUPS, COLS * SLOTS), f32),
            vmem((2 * OWN * TILE, DEPTH), bf16),
            vmem((2 * TILE, LANES), f32),
            vmem((CHUNKS, 2, TILE, LANES), f32),
            vmem((CHUNKS, 2, TILE, LANES), f32),
            vmem((CHUNKS, LONG, TILE, LANES), bf16),
            vmem((CHUNKS, LONG, TILE, LANES), bf16),
            vmem((CHUNKS, SHORT, TILE, LANES), bf16),
            vmem((CHUNKS, SHORT, TILE, LANES), bf16),
            dma((3,)),
            dma((PEERS,)),
            dma((PEERS,)),
            dma((CHUNKS, PEERS)),
            dma((CHUNKS, PEERS)),
            dma((CHUNKS,)),
            dma((CHUNKS,)),
            dma((CHUNKS, LONG)),
            dma((CHUNKS, LONG)),
            dma((CHUNKS, SHORT)),
            dma((CHUNKS, SHORT)),
        ],
        compiler_params=pltpu.CompilerParams(
            collective_id=0, has_side_effects=True, vmem_limit_bytes=56 * 1024 * 1024
        ),
        cost_estimate=pl.CostEstimate(flops=6 * 10**9, bytes_accessed=10 * 2**20, transcendentals=0),
    )(order, table, kernel_v, kernel_u, sources, target)


def solution(mesh):
    return jax.shard_map(
        on_device,
        mesh=mesh,
        in_specs=(
            P("freq", None, "tcol", None, None, None),
            P("freq", "tcol", None, None, None, None),
            P("freq", None, "tcol", None),
            P("freq", None, "tcol"),
            P(),
        ),
        out_specs=P("freq", "tcol", None, None),
        check_vma=False,
    )
```

time: 216 us -> 106 us (0.49); the launches traced: 216 us -> 104 us
  waiting for transfers between devices: 139 us -> 0 us
  Pallas kernels: 0 us -> 97.1 us
  other arithmetic: 22 us -> 3.11 us
  local copies, waits for them, and re-layouts: 19.8 us -> 3.32 us
  matrix products: 14.1 us -> 0 us
  between operations: 13.5 us -> 0.07 us
  starting transfers between devices: 7.7 us -> 0 us
    pallas_call x0 -> x1, Pallas kernels: none -> 97.1 us  [on_device(): pl.pallas_call(kernel, out_shape=jax.ShapeDtypeStruct((1, OWN, TILE, WIDT...]
    reduce_scatter x1 -> x0, waiting for transfers between devices: 85 us -> none  [on_device(): lax.psum_scatter(cos_col * y_real[None] - sin_col * y_imag[None], 'freq',...]
    all_to_all x1 -> x0, waiting for transfers between devices: 54 us -> none  [on_device(): lax.all_to_all(outgoing, 'tcol', split_axis=0, concat_axis=2, tiled=True)[0]]
    dot_general x2 -> x0, matrix products: 14.1 us -> none  [the longest x1 9.22 us: on_device(): jnp.einsum('qjart,qjbrs->qabts', kernel_u[0], arrived, preferred_element_...]
    all_to_all x1 -> x0, starting transfers between devices: 7.48 us -> none  [on_device(): lax.all_to_all(outgoing, 'tcol', split_axis=0, concat_axis=2, tiled=True)[0]]
    sub x3 -> x0, other arithmetic: 7.46 us -> none  [the longest x1 4.42 us: on_device(): cos_col * y_real[None] - sin_col * y_imag[None]]
    all_to_all x1 -> x0, local copies, waits for them, and re-layouts: 7.39 us -> none  [on_device(): lax.all_to_all(outgoing, 'tcol', split_axis=0, concat_axis=2, tiled=True)[0]]
    squeeze x1 -> x0, local copies, waits for them, and re-layouts: 6.93 us -> none  [on_device(): lax.all_to_all(outgoing, 'tcol', split_axis=0, concat_axis=2, tiled=True)[0]]
  transfers between devices with their start and end apart: 2 -> 0, of which waited for: 2 -> 0; matrix products, arithmetic and copies ran while one was open for 0% -> 0% of each run, Pallas kernels for 0% -> 0%
where the time goes in v1:
time: 106 us; the launch traced here: 104 us
  Pallas kernels  97.1 us (92%)
  local copies, waits for them, and re-layouts  3.32 us (3%)
  other arithmetic  3.11 us (3%)
    pallas_call x1, Pallas kernels, on_device(): pl.pallas_call(kernel, out_shape=jax.ShapeDtypeStruct((1, OWN, TILE, WIDT...  97.1 us

profile of v1, /device:TPU:2, one launch (start us, length us, event | category | flops | bytes accessed | tf_op | source)
XLA Modules:
  0.0 103.6 jit_solution(5547908035695910406)
XLA Ops:
  0.0 0.7 iota_add_fusion.1
  0.7 0.2 convert_reduce_fusion
  0.8 0.6 select_reduce_fusion.2.order
  1.5 0.1 lt.72
  1.6 0.8 select_reduce_fusion
  2.4 0.1 mul.47
  2.5 0.1 cosine_multiply_fusion
  2.6 0.6 pad_maximum_fusion.table
  3.2 0.1 copy.8
  3.3 0.1 lt.74
  3.4 0.1 copy.9
  3.4 0.1 select_reduce_fusion.1
  3.5 0.1 copy.10
  3.6 0.1 add.42
  3.7 0.1 add.43
  3.8 0.1 lt.75
  3.9 0.1 lt.76
  4.0 0.6 pad.4.tgt
  4.6 97.1 %shard_map.55 = f32[1,2,256,256]{3,2,1,0:T(8,128)} custom-call(s32[32]{0:T(128)} %select_reduce_fusion.2.order, f32[512]{0:T(512)} %pad_maximum_fusion.table, bf16[1,32,4,2,32,256]{5,4,3,2,1,0:T(8,128)(2,1)} %v_hbm.1, bf16[1,2,64,2,32,256]{5,4,3,2,1,0:T(8,128)(2,1)} %u_hbm.1, bf16[1,2,1024,256]{3,2,1,0:T(8,128)(2,1)} %x_hbm.1, f32[16,8,128]{2,1,0:T(8,128)} %pad.4.tgt), custom_call_target="tpu_custom_call" | custom-call | flops 6000000000 | bytes 10485760 | tf_op jit(solution)/shard_map/pallas_call | solution.py:253
  101.7 1.9 %copy.12 = f32[1,2,256,256]{3,2,1,0:T(8,128)} copy(f32[1,2,256,256]{3,2,1,0:T(8,128)} %shard_map.55) | data formatting | bytes 1048576
  (7 shorter events, 0.1 us)

commit v2 on v1

v2 whole, which is shorter than its diff:
```python
import jax
import jax.numpy as jnp
import numpy as np
from jax import lax
from jax.experimental import pallas as pl
from jax.experimental.pallas import tpu as pltpu
from jax.sharding import PartitionSpec as P

MESH = pl.DeviceIdType.MESH
NX, NY, NZ = 4, 4, 8
GROUPS = NX * NY
ROWS, COLS, SLOTS, TILE, WIDTH = 32, 4, 32, 256, 256
OWN = ROWS // GROUPS
PACK = 192
CHUNKS = 4
HALF = WIDTH // CHUNKS
LANES = 2 * HALF
DEPTH = GROUPS * PACK
BANDS = 2
BAND = TILE // BANDS

OFFSETS = (
    (2, 2), (2, 1), (1, 2), (2, 3), (3, 2), (1, 1), (3, 3), (1, 3), (3, 1),
    (2, 0), (0, 2), (1, 0), (3, 0), (0, 1), (0, 3),
)
PEERS = len(OFFSETS)


def swap_halves(v):
    return pltpu.roll(v, HALF, 1)


def kernel(
    owners, ranks, table, v_hbm, u_hbm, x_hbm, out,
    order, tgt, v, u, x, xs, coeff, packed, arrived, heads, left, acc,
    mine, theirs, near_out, near_in, far_out, far_in,
    load_sem, head_send, head_recv, tile_send, tile_recv, pair_send, pair_recv,
    near_send, near_recv, far_send, far_recv,
):
    freq, here = lax.axis_index("freq"), lax.axis_index("tcol")
    z, core = freq // 2, freq % 2
    px, py = here // NY, here % NY

    def load_v(j):
        return pltpu.make_async_copy(v_hbm.at[0, :, j], v.at[j], load_sem.at[2 + j])

    load_x = pltpu.make_async_copy(x_hbm.at[0], x, load_sem.at[0])
    load_u = pltpu.make_async_copy(u_hbm.at[0], u, load_sem.at[1])
    load_x.start()
    for j in range(COLS):
        load_v(j).start()
    load_u.start()

    def peer(k):
        dx, dy = OFFSETS[k]
        return ((px + dx) % NX) * NY + (py + dy) % NY

    sibling = (2 * z + 1 - core, here)
    sigma = 1 - 2 * core

    def along(steps):
        return (2 * ((z + sigma * steps + NZ) % NZ) + core, here)

    barrier = pltpu.get_barrier_semaphore()
    partners = [(freq, peer(k)) for k in range(PEERS)] + [sibling]
    partners += [along(steps) for steps in (1, -1, 2, -2, 3, -3)]
    for partner in partners:
        pl.semaphore_signal(barrier, inc=1, device_id=partner, device_id_type=MESH)

    def remote(src, dst, send, recv, device):
        return pltpu.make_async_remote_copy(
            src_ref=src, dst_ref=dst, send_sem=send, recv_sem=recv,
            device_id=device, device_id_type=MESH,
        )

    sub = lax.broadcasted_iota(jnp.int32, (8, COLS * SLOTS), 0)
    lane = lax.broadcasted_iota(jnp.int32, (8, COLS * SLOTS), 1)
    slot, column = lane % SLOTS, lane // SLOTS

    @pl.loop(0, GROUPS)
    def _(o):
        low, high = jnp.int32(ROWS - 1), jnp.int32(0)
        for i in range(ROWS):
            hit = owners[i] == o
            low = jnp.minimum(low, jnp.where(hit, i, ROWS - 1))
            high = jnp.maximum(high, jnp.where(hit, i, 0))
        start = jnp.int32(0)
        place = jnp.full((8, COLS * SLOTS), -1000, jnp.int32)
        for q, row in enumerate((low, high)):
            order[OWN * o + q] = row
            for j in range(COLS):
                rank = ranks[j, row]
                live = (sub == q) & (column == j) & (slot < rank)
                place = jnp.where(live, slot + start, place)
                start += rank
        tgt[o] = place.astype(jnp.float32)

    first = lax.broadcasted_iota(jnp.int32, (TILE, LANES), 1) < HALF
    rank_row = lax.broadcasted_iota(jnp.int32, (PACK, COLS * SLOTS), 0).astype(jnp.float32)
    my_rows = pl.ds(pl.multiple_of(PACK * here, PACK), PACK)
    head_rows = pl.ds(pl.multiple_of(8 * here, 8), 8)

    def head_copy(k):
        return remote(tgt.at[peer(k)], heads.at[head_rows], head_send.at[k], head_recv.at[k], (freq, peer(k)))

    def tile_copy(c, k):
        return remote(
            packed.at[c, k], arrived.at[c, my_rows], tile_send.at[c, k], tile_recv.at[c, k], (freq, peer(k))
        )

    def pack(owner):
        total = None
        for q in range(OWN):
            pick = jnp.where(rank_row == tgt[owner, q : q + 1, :], 1.0, 0.0).astype(jnp.bfloat16)
            part = jnp.dot(pick, coeff[order[OWN * owner + q]], preferred_element_type=jnp.float32)
            total = part if total is None else total + part
        return total.astype(jnp.bfloat16)

    load_x.wait()
    for half in range(CHUNKS // 2):
        lanes = pl.ds(half * LANES, LANES)

        @pl.loop(0, COLS)
        def _(j):
            rows = pl.ds(pl.multiple_of(j * TILE, TILE), TILE)
            re = x[0, rows, lanes].astype(jnp.float32)
            im = x[1, rows, lanes].astype(jnp.float32)
            re_swap, im_swap = swap_halves(re), swap_halves(im)
            xs[j, 0, :, :LANES] = jnp.where(first, re, im_swap).astype(jnp.bfloat16)
            xs[j, 0, :, LANES:] = jnp.where(first, re_swap, im).astype(jnp.bfloat16)
            xs[j, 1, :, :LANES] = jnp.where(first, im, -re_swap).astype(jnp.bfloat16)
            xs[j, 1, :, LANES:] = jnp.where(first, im_swap, -re).astype(jnp.bfloat16)

        @pl.loop(0, COLS)
        def _(j):
            if half == 0:
                load_v(j).wait()
            slot_rows = pl.ds(pl.multiple_of(j * SLOTS, SLOTS), SLOTS)
            for part in range(2):
                rows = pl.ds(part * (ROWS // 2), ROWS // 2)
                re = v[j, rows, 0].reshape(ROWS // 2 * SLOTS, TILE)
                im = v[j, rows, 1].reshape(ROWS // 2 * SLOTS, TILE)
                prod = jnp.dot(re, xs[j, 0], preferred_element_type=jnp.float32)
                prod += jnp.dot(im, xs[j, 1], preferred_element_type=jnp.float32)
                coeff[rows, slot_rows, :] = prod.astype(jnp.bfloat16).reshape(ROWS // 2, SLOTS, 2 * LANES)

        if half == 0:
            pl.semaphore_wait(barrier, len(partners))
        for k in range(PEERS):
            block = pack(peer(k))
            packed[2 * half, k] = block[:, :LANES]
            packed[2 * half + 1, k] = block[:, LANES:]
            tile_copy(2 * half, k).start()
        if half == 0:
            for k in range(PEERS):
                head_copy(k).start()
            heads[head_rows] = tgt[here]
        for k in range(PEERS):
            tile_copy(2 * half + 1, k).start()
        block = pack(here)
        arrived[2 * half, my_rows] = block[:, :LANES]
        arrived[2 * half + 1, my_rows] = block[:, LANES:]

    for k in range(PEERS):
        head_copy(k).wait_recv()
    load_u.wait()
    columns = jnp.transpose(heads[...])
    pair_row = lax.broadcasted_iota(jnp.int32, (COLS * SLOTS, 2 * PACK), 1).astype(jnp.float32)
    for e in range(GROUPS // 2):
        for q in range(OWN):
            sides = []
            for side in range(2):
                at = 8 * (2 * e + side) + q
                places = columns[:, at : at + 1] + float(side * PACK)
                sides.append(jnp.where(pair_row == places, 1.0, 0.0).astype(jnp.bfloat16))
            pick = jnp.concatenate(sides, axis=0)
            for a in range(2):
                block = u[q, 2 * COLS * e : 2 * COLS * (e + 1), a].reshape(2 * COLS * SLOTS, TILE)
                turned = lax.dot_general(block, pick, (((0,), (0,)), ((), ())), preferred_element_type=jnp.float32)
                turned = turned.astype(jnp.bfloat16)
                at = (2 * q + a) * BAND
                for t in range(BANDS):
                    left[t, at : at + BAND, 2 * PACK * e : 2 * PACK * (e + 1)] = turned[t * BAND : (t + 1) * BAND]

    head = first[:BAND]

    def pair_copy(c, t):
        return remote(mine.at[c, t], theirs.at[c, t], pair_send.at[c, t], pair_recv.at[c, t], sibling)

    def near_copy(c, t, n):
        rows, steps = ((pl.ds(0, 2), 1), (pl.ds(2, 1), -1), (pl.ds(3, 1), -1))[n]
        return remote(
            near_out.at[c, t, rows], near_in.at[c, t, rows], near_send.at[c, t, n], near_recv.at[c, t, n], along(steps)
        )

    def far_copy(c, t, n):
        return remote(
            far_out.at[c, t, n], far_in.at[c, t, n], far_send.at[c, t, n], far_recv.at[c, t, n], along((3, 1, -2)[n])
        )

    def share(c, t, steps):
        at = along(steps)[0] * (2 * NZ)
        own, other = at + freq, at + 2 * z + 1 - core
        shift = 4 * NZ * NZ
        return (
            table[own] * mine[c, t, 0] - table[own + shift] * mine[c, t, 1]
            + table[other] * theirs[c, t, 0] - table[other + shift] * theirs[c, t, 1]
        )

    def fields(c, t):
        acc[...] = jnp.dot(left[t], arrived[c], preferred_element_type=jnp.float32)
        parts = []
        for q in range(OWN):
            turned = swap_halves(acc[(2 * q + 1) * BAND : (2 * q + 2) * BAND])
            parts.append(acc[2 * q * BAND : (2 * q + 1) * BAND] + jnp.where(head, -turned, turned))
        mine[c, t, 0] = jnp.where(head, parts[0], swap_halves(parts[1]))
        mine[c, t, 1] = jnp.where(head, swap_halves(parts[0]), parts[1])
        pair_copy(c, t).start()

    def to_near(c, t):
        pair_copy(c, t).wait_recv()
        for n, steps in enumerate((4, 2, -3, -1)):
            near_out[c, t, n] = share(c, t, steps).astype(jnp.bfloat16)
            if n:
                near_copy(c, t, n - 1).start()

    def to_far(c, t):
        near_copy(c, t, 0).wait_recv()
        near_copy(c, t, 1).wait_recv()
        for n, steps in enumerate((3, 1, -2)):
            total = share(c, t, steps) + near_in[c, t, n].astype(jnp.float32)
            far_out[c, t, n] = total.astype(jnp.bfloat16)
            far_copy(c, t, n).start()

    def finish(c, t):
        near_copy(c, t, 2).wait_recv()
        total = share(c, t, 0) + near_in[c, t, 3].astype(jnp.float32)
        for n in (1, 2, 0):
            far_copy(c, t, n).wait_recv()
            total += far_in[c, t, n].astype(jnp.float32)
        turned = swap_halves(total)
        at = c * HALF
        rows = slice(t * BAND, (t + 1) * BAND)
        if c % 2 == 0:
            out[0, 0, rows, at : at + HALF] = total[:, :HALF]
            out[0, 1, rows, at : at + HALF] = turned[:, :HALF]
        else:
            out[0, 0, rows, at : at + HALF] = turned[:, HALF:]
            out[0, 1, rows, at : at + HALF] = total[:, HALF:]

    for c in range(CHUNKS):
        for k in range(PEERS):
            tile_copy(c, k).wait_recv()
        for t in range(BANDS):
            fields(c, t)
        for t in range(BANDS):
            to_near(c, t)
        for t in range(BANDS):
            if c:
                finish(c - 1, t)
        for t in range(BANDS):
            to_far(c, t)
    for t in range(BANDS):
        finish(CHUNKS - 1, t)

    for c in range(CHUNKS):
        for k in range(PEERS):
            tile_copy(c, k).wait_send()
        for t in range(BANDS):
            pair_copy(c, t).wait_send()
            for n in range(3):
                near_copy(c, t, n).wait_send()
                far_copy(c, t, n).wait_send()
    for k in range(PEERS):
        head_copy(k).wait_send()


def on_device(kernel_v, kernel_u, sources, ranks, row_owner):
    count = 2 * NZ
    phase = (np.arange(1, count + 1)[None, :] * np.arange(count)[:, None]) % (2 * count)
    angle = np.float32(np.pi) * phase.astype(np.float32) / np.float32(count)
    scale = np.float32(count ** (-0.5))
    table = np.concatenate([(np.cos(angle) * scale).reshape(-1), (np.sin(angle) * scale).reshape(-1)])

    bf16, f32 = jnp.bfloat16, jnp.float32
    vmem, dma = pltpu.VMEM, pltpu.SemaphoreType.DMA
    scalars = pl.BlockSpec(memory_space=pltpu.SMEM)
    away = pl.BlockSpec(memory_space=pl.ANY)
    rows, cols, parts, slots, tile = kernel_v.shape[1:]
    return pl.pallas_call(
        kernel,
        out_shape=jax.ShapeDtypeStruct((1, OWN, TILE, WIDTH), f32),
        in_specs=[scalars, scalars, scalars, away, away, away],
        out_specs=pl.BlockSpec(memory_space=pltpu.VMEM),
        scratch_shapes=[
            pltpu.SMEM((ROWS,), jnp.int32),
            vmem((GROUPS, 8, COLS * SLOTS), f32),
            vmem((cols, rows, parts, slots, tile), bf16),
            vmem(kernel_u.shape[1:], bf16),
            vmem(sources.shape[1:], bf16),
            vmem((COLS, 2, TILE, 2 * LANES), bf16),
            vmem((ROWS, COLS * SLOTS, 2 * LANES), bf16),
            vmem((CHUNKS, PEERS, PACK, LANES), bf16),
            vmem((CHUNKS, DEPTH, LANES), bf16),
            vmem((8 * GROUPS, COLS * SLOTS), f32),
            vmem((BANDS, 2 * OWN * BAND, DEPTH), bf16),
            vmem((2 * OWN * BAND, LANES), f32),
            vmem((CHUNKS, BANDS, 2, BAND, LANES), f32),
            vmem((CHUNKS, BANDS, 2, BAND, LANES), f32),
            vmem((CHUNKS, BANDS, 4, BAND, LANES), bf16),
            vmem((CHUNKS, BANDS, 4, BAND, LANES), bf16),
            vmem((CHUNKS, BANDS, 3, BAND, LANES), bf16),
            vmem((CHUNKS, BANDS, 3, BAND, LANES), bf16),
            dma((2 + COLS,)),
            dma((PEERS,)),
            dma((PEERS,)),
            dma((CHUNKS, PEERS)),
            dma((CHUNKS, PEERS)),
            dma((CHUNKS, BANDS)),
            dma((CHUNKS, BANDS)),
            dma((CHUNKS, BANDS, 3)),
            dma((CHUNKS, BANDS, 3)),
            dma((CHUNKS, BANDS, 3)),
            dma((CHUNKS, BANDS, 3)),
        ],
        compiler_params=pltpu.CompilerParams(
            collective_id=0, has_side_effects=True, vmem_limit_bytes=56 * 1024 * 1024
        ),
        cost_estimate=pl.CostEstimate(flops=6 * 10**9, bytes_accessed=10 * 2**20, transcendentals=0),
    )(row_owner, jnp.transpose(ranks[0]), table, kernel_v, kernel_u, sources)


def solution(mesh):
    return jax.shard_map(
        on_device,
        mesh=mesh,
        in_specs=(
            P("freq", None, "tcol", None, None, None),
            P("freq", "tcol", None, None, None, None),
            P("freq", None, "tcol", None),
            P("freq", None, "tcol"),
            P(),
        ),
        out_specs=P("freq", "tcol", None, None),
        check_vma=False,
    )
```

time: 106 us -> 81.3 us (0.77); the launches traced: 104 us -> 80.2 us
  Pallas kernels: 97.1 us -> 78.4 us
  other arithmetic: 3.11 us -> 0 us
  local copies, waits for them, and re-layouts: 3.32 us -> 1.87 us
    pallas_call x1, Pallas kernels: 97.1 us -> 78.4 us  [on_device(): pl.pallas_call(kernel, out_shape=jax.ShapeDtypeStruct((1, OWN, TILE, WIDT...]
    reduce_sum x4 -> x0, other arithmetic: 1.72 us -> none  [the longest x1 0.82 us: on_device(): slotted = jnp.sum(jnp.where(placed[:, :, None], ranks[0][None], 0), axis=1)]
where the time goes in v2:
time: 81.3 us; the launch traced here: 80.2 us
  Pallas kernels  78.4 us (96%)
  local copies, waits for them, and re-layouts  1.87 us (2%)
    pallas_call x1, Pallas kernels, on_device(): pl.pallas_call(kernel, out_shape=jax.ShapeDtypeStruct((1, OWN, TILE, WIDT...  78.4 us
    unnamed x1, local copies, waits for them, and re-layouts  1.87 us

profile of v2, /device:TPU:2, one launch (start us, length us, event | category | flops | bytes accessed | tf_op | source)
XLA Modules:
  0.0 80.2 jit_solution(3739692548103493889)
XLA Ops:
  0.0 78.4 %shard_map.64 = f32[1,2,256,256]{3,2,1,0:T(8,128)} custom-call(s32[32]{0:T(128)} %owners.1, s32[4,32]{1,0:T(4,128)} %bitcast.3, f32[512]{0:T(512)} %constant.2.clone.table, bf16[1,32,4,2,32,256]{5,4,3,2,1,0:T(8,128)(2,1)} %v_hbm.1, bf16[1,2,64,2,32,256]{5,4,3,2,1,0:T(8,128)(2,1)} %u_hbm.1, bf16[1,2,1024,256]{3,2,1,0:T(8,128)(2,1)} %x_hbm.1), custom_call_target="tpu_custom_call" | custom-call | flops 6000000000 | bytes 10485760 | tf_op jit(solution)/shard_map/pallas_call | solution.py:290
  78.4 1.9 %copy.8 = f32[1,2,256,256]{3,2,1,0:T(8,128)} copy(f32[1,2,256,256]{3,2,1,0:T(8,128)} %shard_map.64) | data formatting | bytes 1048576

commit v3 on v2

--- a/solution.py
+++ b/solution.py
@@ -254,12 +254,17 @@
         for t in range(BANDS):
             fields(c, t)
         for t in range(BANDS):
+            if c:
+                to_far(c - 1, t)
+        for t in range(BANDS):
             to_near(c, t)
         for t in range(BANDS):
-            if c:
-                finish(c - 1, t)
-        for t in range(BANDS):
-            to_far(c, t)
+            if c > 1:
+                finish(c - 2, t)
+    for t in range(BANDS):
+        finish(CHUNKS - 2, t)
+    for t in range(BANDS):
+        to_far(CHUNKS - 1, t)
     for t in range(BANDS):
         finish(CHUNKS - 1, t)
 

time: 81.3 us -> 79.5 us (0.978)
  Pallas kernels: 78.4 us -> 76.1 us
    pallas_call x1, Pallas kernels: 78.4 us -> 76.1 us  [on_device(): pl.pallas_call(kernel, out_shape=jax.ShapeDtypeStruct((1, OWN, TILE, WIDT...]
where the time goes in v3:
time: 79.5 us; the launch traced here: 78 us
  Pallas kernels  76.1 us (96%)
  local copies, waits for them, and re-layouts  1.87 us (2%)
    pallas_call x1, Pallas kernels, on_device(): pl.pallas_call(kernel, out_shape=jax.ShapeDtypeStruct((1, OWN, TILE, WIDT...  76.1 us
    unnamed x1, local copies, waits for them, and re-layouts  1.87 us

profile of v3, /device:TPU:2, one launch (start us, length us, event | category | flops | bytes accessed | tf_op | source)
XLA Modules:
  0.0 78.0 jit_solution(11065998314253149618)
XLA Ops:
  0.0 76.1 %shard_map.64 = f32[1,2,256,256]{3,2,1,0:T(8,128)} custom-call(s32[32]{0:T(128)} %owners.1, s32[4,32]{1,0:T(4,128)} %bitcast.3, f32[512]{0:T(512)} %constant.2.clone.table, bf16[1,32,4,2,32,256]{5,4,3,2,1,0:T(8,128)(2,1)} %v_hbm.1, bf16[1,2,64,2,32,256]{5,4,3,2,1,0:T(8,128)(2,1)} %u_hbm.1, bf16[1,2,1024,256]{3,2,1,0:T(8,128)(2,1)} %x_hbm.1), custom_call_target="tpu_custom_call" | custom-call | flops 6000000000 | bytes 10485760 | tf_op jit(solution)/shard_map/pallas_call | solution.py:295
  76.1 1.9 %copy.8 = f32[1,2,256,256]{3,2,1,0:T(8,128)} copy(f32[1,2,256,256]{3,2,1,0:T(8,128)} %shard_map.64) | data formatting | bytes 1048576

commit v4 on v3

--- a/solution.py
+++ b/solution.py
@@ -16,7 +16,7 @@
 HALF = WIDTH // CHUNKS
 LANES = 2 * HALF
 DEPTH = GROUPS * PACK
-BANDS = 2
+BANDS = 4
 BAND = TILE // BANDS
 
 OFFSETS = (

time: 79.5 us -> 77.7 us (0.977)
  Pallas kernels: 76.1 us -> 74.9 us
    pallas_call x1, Pallas kernels: 76.1 us -> 74.9 us  [on_device(): pl.pallas_call(kernel, out_shape=jax.ShapeDtypeStruct((1, OWN, TILE, WIDT...]
where the time goes in v4:
time: 77.7 us; the launch traced here: 76.8 us
  Pallas kernels  74.9 us (96%)
  local copies, waits for them, and re-layouts  1.87 us (2%)
    pallas_call x1, Pallas kernels, on_device(): pl.pallas_call(kernel, out_shape=jax.ShapeDtypeStruct((1, OWN, TILE, WIDT...  74.9 us
    unnamed x1, local copies, waits for them, and re-layouts  1.87 us

profile of v4, /device:TPU:2, one launch (start us, length us, event | category | flops | bytes accessed | tf_op | source)
XLA Modules:
  0.0 76.8 jit_solution(1831380094757787227)
XLA Ops:
  0.0 74.9 %shard_map.64 = f32[1,2,256,256]{3,2,1,0:T(8,128)} custom-call(s32[32]{0:T(128)} %owners.1, s32[4,32]{1,0:T(4,128)} %bitcast.3, f32[512]{0:T(512)} %constant.2.clone.table, bf16[1,32,4,2,32,256]{5,4,3,2,1,0:T(8,128)(2,1)} %v_hbm.1, bf16[1,2,64,2,32,256]{5,4,3,2,1,0:T(8,128)(2,1)} %u_hbm.1, bf16[1,2,1024,256]{3,2,1,0:T(8,128)(2,1)} %x_hbm.1), custom_call_target="tpu_custom_call" | custom-call | flops 6000000000 | bytes 10485760 | tf_op jit(solution)/shard_map/pallas_call | solution.py:295
  74.9 1.9 %copy.8 = f32[1,2,256,256]{3,2,1,0:T(8,128)} copy(f32[1,2,256,256]{3,2,1,0:T(8,128)} %shard_map.64) | data formatting | bytes 1048576

commit v5 on v4

--- a/solution.py
+++ b/solution.py
@@ -251,20 +251,23 @@
     for c in range(CHUNKS):
         for k in range(PEERS):
             tile_copy(c, k).wait_recv()
-        for t in range(BANDS):
+        ready = BANDS // 2 if c == CHUNKS - 1 else BANDS
+        for t in range(ready):
             fields(c, t)
         for t in range(BANDS):
             if c:
                 to_far(c - 1, t)
         for t in range(BANDS):
             to_near(c, t)
+            if ready + t < BANDS:
+                fields(c, ready + t)
         for t in range(BANDS):
             if c > 1:
                 finish(c - 2, t)
     for t in range(BANDS):
+        to_far(CHUNKS - 1, t)
+    for t in range(BANDS):
         finish(CHUNKS - 2, t)
-    for t in range(BANDS):
-        to_far(CHUNKS - 1, t)
     for t in range(BANDS):
         finish(CHUNKS - 1, t)
 

time: 77.7 us -> 77.9 us (level)
  no operation moved by 1% of the time
where the time goes in v5:
time: 77.9 us; the launch traced here: 77.1 us
  Pallas kernels  75.2 us (97%)
  local copies, waits for them, and re-layouts  1.87 us (2%)
    pallas_call x1, Pallas kernels, on_device(): pl.pallas_call(kernel, out_shape=jax.ShapeDtypeStruct((1, OWN, TILE, WIDT...  75.2 us
    unnamed x1, local copies, waits for them, and re-layouts  1.87 us

profile of v5, /device:TPU:2, one launch (start us, length us, event | category | flops | bytes accessed | tf_op | source)
XLA Modules:
  0.0 77.1 jit_solution(4052671942393401179)
XLA Ops:
  0.0 75.2 %shard_map.64 = f32[1,2,256,256]{3,2,1,0:T(8,128)} custom-call(s32[32]{0:T(128)} %owners.1, s32[4,32]{1,0:T(4,128)} %bitcast.3, f32[512]{0:T(512)} %constant.2.clone.table, bf16[1,32,4,2,32,256]{5,4,3,2,1,0:T(8,128)(2,1)} %v_hbm.1, bf16[1,2,64,2,32,256]{5,4,3,2,1,0:T(8,128)(2,1)} %u_hbm.1, bf16[1,2,1024,256]{3,2,1,0:T(8,128)(2,1)} %x_hbm.1), custom_call_target="tpu_custom_call" | custom-call | flops 6000000000 | bytes 10485760 | tf_op jit(solution)/shard_map/pallas_call | solution.py:298
  75.2 1.9 %copy.8 = f32[1,2,256,256]{3,2,1,0:T(8,128)} copy(f32[1,2,256,256]{3,2,1,0:T(8,128)} %shard_map.64) | data formatting | bytes 1048576
